TPU v7x, 128 devices: a whole 4x4x4 slice. The times are simulated.
128 devices in a mesh: ctx: 16 (over z_lo, y, core), section: 8 (over z_hi, x).
Axes of the slice: x: 4, y: 4, z: 4 (z_hi: 2, z_lo: 2; z = z_hi * 2 + z_lo), core: 2. Of those that a mesh axis runs over, the one named last changes fastest.
Arguments:
- queries: bfloat16 [8, 2048, 4096], P('section', 'ctx'), may hold values from -39 to 39, as said below
- key_vectors: bfloat16 [8, 2048, 512], P('section', 'ctx'), may hold values from -6 to 6
- value_vectors: bfloat16 [8, 2048, 512], P('section', 'ctx'), may hold values from -6 to 6
- cotangent: bfloat16 [8, 2048, 4096], P('section', 'ctx'), may hold values from -6 to 6
- slot_order: int32 [32], replicated, may hold values from 0 to 31, each once
Outputs:
- handed: bfloat16 [8, 2048, 4096], P('section', 'ctx')
- grad_query: bfloat16 [8, 2048, 4096], P('section', 'ctx')
- grad_key: float32 [8, 2048, 512], P('section', 'ctx')
- grad_value: float32 [8, 2048, 512], P('section', 'ctx')
Inputs may be any that keep to these rules, and one draw needn't show every extreme that they name: `queries`: query entries lie in the stated range. slot_order is a permutation of the 32 blocks of the sequence.
All inputs are finite; a program needn't handle non-finite values.
Results may differ from a plain program's by a relative error of at most 0.017.
Values may be sent and summed in bfloat16 or wider, within the bound.
No kernel may reach another device: no remote copies, remote signals or barrier semaphores. Data moves between devices by JAX's collectives and lax.ppermute only.
A program may use at most 128 MiB of HBM per device.

v0:
```python
import math

import jax
import jax.numpy as jnp
from jax import lax
from jax.sharding import PartitionSpec as P

BLK = 64
HEADS = 32
KV_HEADS = 4
HEAD_DIM = 128


masked_score = -1e30


def from_behind(block, axis, distance):
    devices = range(lax.axis_size(axis))
    route = [((i - distance) % len(devices), i) for i in devices]
    return lax.ppermute(block, axis, route)


def positions_of(slot_order, first_row, row_count):
    row_ids = first_row + jnp.arange(row_count, dtype=jnp.int32)
    block_ids = jnp.arange(slot_order.shape[0], dtype=jnp.int32)
    matches = (row_ids // BLK)[:, None] == block_ids[None, :]
    first_pos = jnp.sum(jnp.where(matches, slot_order[None, :], 0), axis=1)
    return first_pos * BLK + row_ids % BLK


def stats_block(running, key_local, first_row, query_heads, query_pos, slot_order):
    row_count = key_local.shape[0]
    score_scale = 1.0 / math.sqrt(HEAD_DIM)
    key_heads = key_local.reshape(row_count, KV_HEADS, HEAD_DIM)
    key_pos = positions_of(slot_order, first_row, row_count)
    visible = (key_pos[None, :] <= query_pos[:, None])[:, None, None, :]

    def stats_update(current):
        highest, denominator = current
        scores = (
            jnp.einsum("rgjd,ngd->rgjn", query_heads, key_heads, preferred_element_type=jnp.float32)
            * score_scale
        )
        scores = jnp.where(visible, scores, masked_score)
        newest = jnp.maximum(highest, jnp.max(scores, axis=-1))
        probabilities = jnp.where(visible, jnp.exp(scores - newest[..., None]), 0.0)
        denominator = jnp.sum(probabilities, axis=-1)
        return (newest, denominator)

    return lax.cond(jnp.any(visible), stats_update, lambda current: current, running)


def body(queries, key_vectors, value_vectors, cotangent, slot_order):
    query_rows = queries[0]
    local_rows = query_rows.shape[0]
    group_size = HEADS // KV_HEADS
    score_scale = 1.0 / math.sqrt(HEAD_DIM)
    cycle_size = lax.axis_size("ctx")
    all_rows = local_rows * cycle_size
    block_rows = local_rows * math.gcd(cycle_size, max(1, 512 // local_rows))
    block_total = all_rows // block_rows
    query_heads = query_rows.reshape(local_rows, KV_HEADS, group_size, HEAD_DIM)
    query_pos = positions_of(slot_order, lax.axis_index("ctx") * local_rows, local_rows)
    key_local = key_vectors[0]
    value_local = value_vectors[0]
    start_state = (
        jnp.full((local_rows, KV_HEADS, group_size), masked_score, jnp.float32),
        jnp.zeros((local_rows, KV_HEADS, group_size), jnp.float32),
    )
    highest, denominator = stats_block(
        start_state,
        lax.all_gather(key_local, "ctx", axis=0, tiled=True),
        jnp.int32(0),
        query_heads,
        query_pos,
        slot_order,
    )
    all_keys, all_values = (
        lax.all_gather(key_local, "ctx", axis=0, tiled=True),
        lax.all_gather(value_local, "ctx", axis=0, tiled=True),
    )
    log_total = highest + jnp.log(denominator)

    def block_inputs(block_index):
        first_row = block_index * block_rows
        key_heads = lax.dynamic_slice_in_dim(all_keys, first_row, block_rows, 0).reshape(
            block_rows, KV_HEADS, HEAD_DIM
        )
        value_heads = lax.dynamic_slice_in_dim(all_values, first_row, block_rows, 0).reshape(
            block_rows, KV_HEADS, HEAD_DIM
        )
        key_pos = positions_of(slot_order, first_row, block_rows)
        visible = (key_pos[None, :] <= query_pos[:, None])[:, None, None, :]
        return (first_row, key_heads, value_heads, visible)

    def normalized(key_heads, visible):
        scores = (
            jnp.einsum("rgjd,ngd->rgjn", query_heads, key_heads, preferred_element_type=jnp.float32)
            * score_scale
        )
        scores = jnp.where(visible, scores, masked_score)
        return jnp.where(visible, jnp.exp(scores - log_total[..., None]), 0.0)

    def attend_step(block_index, weighted):
        first_row, key_heads, value_heads, visible = block_inputs(block_index)

        def attend_update(current):
            weights = normalized(key_heads, visible).astype(jnp.bfloat16)
            return current + jnp.einsum(
                "rgjn,ngd->rgjd", weights, value_heads, preferred_element_type=jnp.float32
            )

        return lax.cond(jnp.any(visible), attend_update, lambda current: current, weighted)

    weighted = lax.fori_loop(
        0,
        block_total,
        attend_step,
        jnp.zeros((local_rows, KV_HEADS, group_size, HEAD_DIM), jnp.float32),
    )
    attended = weighted.astype(jnp.bfloat16)
    handed = from_behind(attended.reshape(local_rows, HEADS * HEAD_DIM), "section", 1)
    grad_rows = from_behind(cotangent[0], "section", -1)
    grad_heads = grad_rows.reshape(local_rows, KV_HEADS, group_size, HEAD_DIM)
    row_delta = jnp.sum(grad_heads.astype(jnp.float32) * attended.astype(jnp.float32), axis=-1)

    def backward_step(block_index, running):
        first_row, key_heads, value_heads, visible = block_inputs(block_index)

        def backward_update(current):
            grad_query, key_terms = current
            probabilities = normalized(key_heads, visible)
            weights = probabilities.astype(jnp.bfloat16)
            grad_probs = jnp.einsum(
                "rgjd,ngd->rgjn", grad_heads, value_heads, preferred_element_type=jnp.float32
            )
            grad_scores = (probabilities * (grad_probs - row_delta[..., None])).astype(jnp.bfloat16)
            grad_query = grad_query + jnp.einsum(
                "rgjn,ngd->rgjd", grad_scores, key_heads, preferred_element_type=jnp.float32
            )
            key_part = (
                jnp.einsum(
                    "rgjn,rgjd->ngd", grad_scores, query_heads, preferred_element_type=jnp.float32
                )
                * score_scale
            )
            value_part = jnp.einsum(
                "rgjn,rgjd->ngd", weights, grad_heads, preferred_element_type=jnp.float32
            )
            stacked = jnp.concatenate(
                [
                    key_part.reshape(block_rows, KV_HEADS * HEAD_DIM),
                    value_part.reshape(block_rows, KV_HEADS * HEAD_DIM),
                ],
                axis=1,
            )
            key_terms = lax.dynamic_update_slice_in_dim(key_terms, stacked, first_row, 0)
            return (grad_query, key_terms)

        return lax.cond(jnp.any(visible), backward_update, lambda current: current, running)

    start_grads = (
        jnp.zeros((local_rows, KV_HEADS, group_size, HEAD_DIM), jnp.float32),
        jnp.zeros((all_rows, 2 * KV_HEADS * HEAD_DIM), jnp.float32),
    )
    grad_query, key_terms = lax.fori_loop(0, block_total, backward_step, start_grads)
    summed = lax.psum_scatter(
        key_terms.astype(jnp.bfloat16), "ctx", scatter_dimension=0, tiled=True
    ).astype(jnp.float32)
    key_width = KV_HEADS * HEAD_DIM
    grad_query = (
        (grad_query * score_scale).astype(jnp.bfloat16).reshape(local_rows, HEADS * HEAD_DIM)
    )
    return (
        handed[None],
        grad_query[None],
        summed[:, :key_width][None],
        summed[:, key_width:][None],
    )


def solution(mesh):
    placed = (
        P("section", "ctx", None),
        P("section", "ctx", None),
        P("section", "ctx", None),
        P("section", "ctx", None),
        P(),
    )
    return jax.shard_map(
        body,
        mesh=mesh,
        in_specs=placed,
        out_specs=(
            P("section", "ctx", None),
            P("section", "ctx", None),
            P("section", "ctx", None),
            P("section", "ctx", None),
        ),
        check_vma=False,
    )
```

profile of v0, /device:TPU:1, one launch (start us, length us, event | category | flops | bytes accessed | tf_op | source)
XLA Modules:
  0.0 298.7 jit_solution(9817449417447324392)
XLA Ops:
  7.2 1.7 copy.105
  8.9 1.7 copy.109
  10.7 6.7 %collective-permute-start.1 = (bf16[128,4096]{1,0:T(8,128)(2,1)}, bf16[128,4096]{1,0:T(8,128)(2,1)}, u32[]{:S(2)}, u32[]{:S(2)}) collective-permute-start(bf16[128,4096]{1,0:T(8,128)(2,1)} %bitcast.134), channel_id=1, source_target_pairs={{1,0},{2,1},{3,2},{4,3},{5,4},{6,5},{7,6},{0,7},{9,8},{10,9},{11,1... | collective-permute-start | bytes 3145736 | tf_op jit(solution)/shard_map/ppermute | solution.py:20
  17.4 1.6 copy.106
  22.2 1.3 copy.110
  23.5 16.1 %collective-permute-done.1 = bf16[128,4096]{1,0:T(8,128)(2,1)} collective-permute-done((bf16[128,4096]{1,0:T(8,128)(2,1)}, bf16[128,4096]{1,0:T(8,128)(2,1)}, u32[]{:S(2)}, u32[]{:S(2)}) %collective-permute-start.1) | collective-permute-done | bytes 1048608 | tf_op jit(solution)/shard_map/ppermute | solution.py:20
  39.6 1.6 copy.113
  41.2 10.0 %all-gather.5.cloned.1.call-done = bf16[1,2048,512]{1,2,0:T(8,128)(2,1)} async-done(((bf16[1,128,512]{1,2,0:T(8,128)(2,1)}), bf16[1,2048,512]{1,2,0:T(8,128)(2,1)}) %all-gather.5.cloned.1.call-update) | async-done | bytes 2097168 | tf_op jit(solution)/shard_map/all_gather | solution.py:79
  51.3 30.4 %conditional.3 = (f32[128,4,8]{0,2,1:T(8,128)}, f32[128,4,8]{0,2,1:T(8,128)S(1)}) conditional(s32[]{:T(128)} %convert_element_type.59, () %tuple.100, (pred[128,1,1,2048]{0,3,2,1:T(8,128)(4,1)S(1)}, bf16[2048,512]{0,1:T(8,128)(2,1)}, bf16[128,4,8,128]{0,3,2,1:T(8,128)(2,1)S(1)}) %tuple.172), branch_computations={%region_3.4_spmd, %region_4.7_spmd} | conditional | flops 2214588416 | bytes 70893584 | solution.py:50
  51.3 14.9 %fusion = (f32[128,4,8]{0,2,1:T(8,128)S(1)}, f32[4,2048,128,8]{2,1,3,0:T(8,128)}) fusion(pred[128,2048]{0,1:T(8,128)(4,1)S(1)} %bitcast.127, bf16[2048,4,128,1]{0,2,3,1:T(8,128)(2,1)} %bitcast.120, bf16[128,4,8,128]{0,3,2,1:T(8,128)(2,1)S(1)} %get-tuple-element.771), kind=kOutput, calls=%fused_computation.2 | convolution fusion | flops 2172645376 | bytes 36978688 | tf_op jit(solution)/shard_map/cond/branch_1_fun/rgjd,ngd->rgjn/dot_general | solution.py:41
  66.8 14.8 %select_reduce_fusion = f32[128,4,8]{0,2,1:T(8,128)S(1)} fusion(f32[4,2048,128,8]{2,1,3,0:T(8,128)} %get-tuple-element.819, f32[128,4,8]{0,2,1:T(8,128)} %broadcast_maximum_fusion, pred[128,2048]{0,1:T(8,128)(4,1)S(1)} %bitcast.128), kind=kLoop, calls=%fused_computation.1 | loop fusion | flops 41938944 | bytes 33849344 | tf_op jit(solution)/shard_map/cond/branch_1_fun/reduce_sum | solution.py:47
  82.4 23.9 %all-gather.7.cloned.1.call-done = bf16[1,2048,512]{1,2,0:T(8,128)(2,1)} async-done(((bf16[1,128,512]{1,2,0:T(8,128)(2,1)}), bf16[1,2048,512]{1,2,0:T(8,128)(2,1)}) %all-gather.7.cloned.1.call-update) | async-done | bytes 2097168 | tf_op jit(solution)/shard_map/all_gather | solution.py:80
  106.3 1.6 broadcast.549.clone
  107.9 39.2 %while.35 = (s32[]{:T(128)}, f32[128,4,8,128]{3,0,2,1:T(8,128)}, s32[32]{0:T(128)S(1)}, s32[128]{0:T(128)S(1)}, bf16[2048,512]{0,1:T(8,128)(2,1)}, /*index=5*/bf...) while((s32[]{:T(128)}, f32[128,4,8,128]{3,0,2,1:T(8,128)}, ...), condition=%wide.region_12.13_spmd, body=%wide.region_7.12_spmd.sunk | while | flops 1084946944 | bytes 8549221 | solution.py:115
  109.4 8.3 %conditional.6 = (f32[128,4,8,128]{3,0,2,1:T(8,128)}) conditional(s32[]{:T(128)} %convert_element_type.78, f32[128,4,8,128]{3,0,2,1:T(8,128)} %get-tuple-element.979, (pred[128,1,1,512]{0,3,2,1:T(8,128)(4,1)S(1)}, s32[]{:T(128)}, bf16[2048,512]{0,1:T(8,128)(2,1)}, bf16[128,4,8,128]{3,0,2,1:T(8,128)(2,1)}, f32[128,4,8]{0,2,1:T(8,128)S(1)}, ...), branch_computations={%region_10.10_spmd, %region_11.11_spmd} | conditional | flops 1084751872 | bytes 8470574 | solution.py:113
  109.5 1.3 constant_dynamic-slice_fusion
  110.7 7.0 %bitcast_add_fusion = f32[128,4,8,128]{3,0,2,1:T(8,128)} fusion(f32[128,4,8,128]{3,0,2,1:T(8,128)} %get-tuple-element.671, bf16[512,4,128,1]{0,2,3,1:T(8,128)(2,1)S(1)} %bitcast.122, f32[128,4,8]{0,2,1:T(8,128)S(1)} %get-tuple-element.676, pred[128,512]{0,1:T(8,128)(4,1)S(1)} %bitcast.133, bf16[512,4,128,1]{0,2,3,1:T(8,128)(2,1)S(1)} %bitcast.123, ...), kind=kOutput, calls=%fused_computation.12 | convolution fusion | flops 1084751872 | bytes 6373376 | tf_op jit(solution)/shard_map/while/body/eval_jaxpr/cond/branch_1_fun/rgjn,ngd->rgjd/dot_general | solution.py:109
  119.2 8.3 %conditional.6 = (f32[128,4,8,128]{3,0,2,1:T(8,128)}) conditional(s32[]{:T(128)} %convert_element_type.78, f32[128,4,8,128]{3,0,2,1:T(8,128)} %get-tuple-element.979, (pred[128,1,1,512]{0,3,2,1:T(8,128)(4,1)S(1)}, s32[]{:T(128)}, bf16[2048,512]{0,1:T(8,128)(2,1)}, bf16[128,4,8,128]{3,0,2,1:T(8,128)(2,1)}, f32[128,4,8]{0,2,1:T(8,128)S(1)}, ...), branch_computations={%region_10.10_spmd, %region_11.11_spmd} | conditional | flops 1084751872 | bytes 8470574 | solution.py:113
  119.3 1.3 constant_dynamic-slice_fusion
  120.5 7.0 %bitcast_add_fusion = f32[128,4,8,128]{3,0,2,1:T(8,128)} fusion(f32[128,4,8,128]{3,0,2,1:T(8,128)} %get-tuple-element.671, bf16[512,4,128,1]{0,2,3,1:T(8,128)(2,1)S(1)} %bitcast.122, f32[128,4,8]{0,2,1:T(8,128)S(1)} %get-tuple-element.676, pred[128,512]{0,1:T(8,128)(4,1)S(1)} %bitcast.133, bf16[512,4,128,1]{0,2,3,1:T(8,128)(2,1)S(1)} %bitcast.123, ...), kind=kOutput, calls=%fused_computation.12 | convolution fusion | flops 1084751872 | bytes 6373376 | tf_op jit(solution)/shard_map/while/body/eval_jaxpr/cond/branch_1_fun/rgjn,ngd->rgjd/dot_general | solution.py:109
  129.0 8.3 %conditional.6 = (f32[128,4,8,128]{3,0,2,1:T(8,128)}) conditional(s32[]{:T(128)} %convert_element_type.78, f32[128,4,8,128]{3,0,2,1:T(8,128)} %get-tuple-element.979, (pred[128,1,1,512]{0,3,2,1:T(8,128)(4,1)S(1)}, s32[]{:T(128)}, bf16[2048,512]{0,1:T(8,128)(2,1)}, bf16[128,4,8,128]{3,0,2,1:T(8,128)(2,1)}, f32[128,4,8]{0,2,1:T(8,128)S(1)}, ...), branch_computations={%region_10.10_spmd, %region_11.11_spmd} | conditional | flops 1084751872 | bytes 8470574 | solution.py:113
  129.1 1.3 constant_dynamic-slice_fusion
  130.4 7.0 %bitcast_add_fusion = f32[128,4,8,128]{3,0,2,1:T(8,128)} fusion(f32[128,4,8,128]{3,0,2,1:T(8,128)} %get-tuple-element.671, bf16[512,4,128,1]{0,2,3,1:T(8,128)(2,1)S(1)} %bitcast.122, f32[128,4,8]{0,2,1:T(8,128)S(1)} %get-tuple-element.676, pred[128,512]{0,1:T(8,128)(4,1)S(1)} %bitcast.133, bf16[512,4,128,1]{0,2,3,1:T(8,128)(2,1)S(1)} %bitcast.123, ...), kind=kOutput, calls=%fused_computation.12 | convolution fusion | flops 1084751872 | bytes 6373376 | tf_op jit(solution)/shard_map/while/body/eval_jaxpr/cond/branch_1_fun/rgjn,ngd->rgjd/dot_general | solution.py:109
  138.9 8.3 %conditional.6 = (f32[128,4,8,128]{3,0,2,1:T(8,128)}) conditional(s32[]{:T(128)} %convert_element_type.78, f32[128,4,8,128]{3,0,2,1:T(8,128)} %get-tuple-element.979, (pred[128,1,1,512]{0,3,2,1:T(8,128)(4,1)S(1)}, s32[]{:T(128)}, bf16[2048,512]{0,1:T(8,128)(2,1)}, bf16[128,4,8,128]{3,0,2,1:T(8,128)(2,1)}, f32[128,4,8]{0,2,1:T(8,128)S(1)}, ...), branch_computations={%region_10.10_spmd, %region_11.11_spmd} | conditional | flops 1084751872 | bytes 8470574 | solution.py:113
  138.9 1.3 constant_dynamic-slice_fusion
  140.2 7.0 %bitcast_add_fusion = f32[128,4,8,128]{3,0,2,1:T(8,128)} fusion(f32[128,4,8,128]{3,0,2,1:T(8,128)} %get-tuple-element.671, bf16[512,4,128,1]{0,2,3,1:T(8,128)(2,1)S(1)} %bitcast.122, f32[128,4,8]{0,2,1:T(8,128)S(1)} %get-tuple-element.676, pred[128,512]{0,1:T(8,128)(4,1)S(1)} %bitcast.133, bf16[512,4,128,1]{0,2,3,1:T(8,128)(2,1)S(1)} %bitcast.123, ...), kind=kOutput, calls=%fused_computation.12 | convolution fusion | flops 1084751872 | bytes 6373376 | tf_op jit(solution)/shard_map/while/body/eval_jaxpr/cond/branch_1_fun/rgjn,ngd->rgjd/dot_general | solution.py:109
  147.1 1.8 copy.111
  149.9 2.4 broadcast_in_dim.235
  152.6 57.8 %while.36 = (s32[]{:T(128)}, f32[128,4,8,128]{3,0,2,1:T(8,128)S(1)}, bf16[2048,1024]{0,1:T(8,128)(2,1)}, s32[32]{0:T(128)S(1)}, s32[128]{0:T(128)S(1)}, /*index=...) while((s32[]{:T(128)}, ...), condition=%wide.region_19.20_spmd, body=%wide.region_14.19_spmd.sunk | while | flops 2712861184 | bytes 57406416 | solution.py:166
  154.4 12.9 %conditional.7 = ((f32[128,4,8,128]{3,0,2,1:T(8,128)S(1)}, bf16[2048,1024]{0,1:T(8,128)(2,1)})) conditional(s32[]{:T(128)} %convert_element_type.79, (f32[128,4,8,128]{3,0,2,1:T(8,128)S(1)}, bf16[2048,1024]{0,1:T(8,128)(2,1)}) %tuple.146, (pred[128,1,1,512]{0,3,2,1:T(8,128)(4,1)S(1)}, s32[]{:T(128)}, bf16[2048,512]{0,1:T(8,128)(2,1)}, ...), branch_computations={%region_17.17_spmd, %region_18.18_spmd} | conditional | flops 2712666112 | bytes 57327708 | solution.py:160
  154.4 1.3 constant_dynamic-slice_fusion.2
  155.7 1.3 fusion.48
  157.0 3.1 %fusion.21 = bf16[128,4,8,512]{0,3,2,1:T(8,128)(2,1)S(1)} fusion(f32[4,512,128,8]{2,1,3,0:T(8,128)S(1)} %fusion.48, f32[128,4,8]{0,2,1:T(8,128)S(1)} %get-tuple-element.695, f32[128,4,8]{0,2,1:T(8,128)S(1)} %get-tuple-element.692, pred[128,512]{0,1:T(8,128)(4,1)S(1)} %bitcast.131, bf16[512,4,128,1]{0,2,3,1:T(8,128)(2,1)S(1)} %bitcast.126, ...), kind=kOutput, calls=%fused_computation.35 | convolution fusion | flops 551550976 | bytes 14254080 | tf_op jit(solution)/shard_map/while/body/eval_jaxpr/cond/branch_1_fun/rgjd,ngd->rgjn/dot_general | solution.py:134
  160.1 1.5 fusion.29
  161.6 2.2 fusion.26
  164.9 2.3 bitcast_add_fusion.1
  168.8 12.8 %conditional.7 = ((f32[128,4,8,128]{3,0,2,1:T(8,128)S(1)}, bf16[2048,1024]{0,1:T(8,128)(2,1)})) conditional(s32[]{:T(128)} %convert_element_type.79, (f32[128,4,8,128]{3,0,2,1:T(8,128)S(1)}, bf16[2048,1024]{0,1:T(8,128)(2,1)}) %tuple.146, (pred[128,1,1,512]{0,3,2,1:T(8,128)(4,1)S(1)}, s32[]{:T(128)}, bf16[2048,512]{0,1:T(8,128)(2,1)}, ...), branch_computations={%region_17.17_spmd, %region_18.18_spmd} | conditional | flops 2712666112 | bytes 57327708 | solution.py:160
  168.8 1.3 constant_dynamic-slice_fusion.2
  170.1 1.3 fusion.48
  171.4 3.1 %fusion.21 = bf16[128,4,8,512]{0,3,2,1:T(8,128)(2,1)S(1)} fusion(f32[4,512,128,8]{2,1,3,0:T(8,128)S(1)} %fusion.48, f32[128,4,8]{0,2,1:T(8,128)S(1)} %get-tuple-element.695, f32[128,4,8]{0,2,1:T(8,128)S(1)} %get-tuple-element.692, pred[128,512]{0,1:T(8,128)(4,1)S(1)} %bitcast.131, bf16[512,4,128,1]{0,2,3,1:T(8,128)(2,1)S(1)} %bitcast.126, ...), kind=kOutput, calls=%fused_computation.35 | convolution fusion | flops 551550976 | bytes 14254080 | tf_op jit(solution)/shard_map/while/body/eval_jaxpr/cond/branch_1_fun/rgjd,ngd->rgjn/dot_general | solution.py:134
  174.5 1.5 fusion.29
  176.0 2.2 fusion.26
  179.3 2.3 bitcast_add_fusion.1
  183.2 12.8 %conditional.7 = ((f32[128,4,8,128]{3,0,2,1:T(8,128)S(1)}, bf16[2048,1024]{0,1:T(8,128)(2,1)})) conditional(s32[]{:T(128)} %convert_element_type.79, (f32[128,4,8,128]{3,0,2,1:T(8,128)S(1)}, bf16[2048,1024]{0,1:T(8,128)(2,1)}) %tuple.146, (pred[128,1,1,512]{0,3,2,1:T(8,128)(4,1)S(1)}, s32[]{:T(128)}, bf16[2048,512]{0,1:T(8,128)(2,1)}, ...), branch_computations={%region_17.17_spmd, %region_18.18_spmd} | conditional | flops 2712666112 | bytes 57327708 | solution.py:160
  183.2 1.3 constant_dynamic-slice_fusion.2
  184.5 1.3 fusion.48
  185.8 3.1 %fusion.21 = bf16[128,4,8,512]{0,3,2,1:T(8,128)(2,1)S(1)} fusion(f32[4,512,128,8]{2,1,3,0:T(8,128)S(1)} %fusion.48, f32[128,4,8]{0,2,1:T(8,128)S(1)} %get-tuple-element.695, f32[128,4,8]{0,2,1:T(8,128)S(1)} %get-tuple-element.692, pred[128,512]{0,1:T(8,128)(4,1)S(1)} %bitcast.131, bf16[512,4,128,1]{0,2,3,1:T(8,128)(2,1)S(1)} %bitcast.126, ...), kind=kOutput, calls=%fused_computation.35 | convolution fusion | flops 551550976 | bytes 14254080 | tf_op jit(solution)/shard_map/while/body/eval_jaxpr/cond/branch_1_fun/rgjd,ngd->rgjn/dot_general | solution.py:134
  188.9 1.5 fusion.29
  190.4 2.2 fusion.26
  193.7 2.3 bitcast_add_fusion.1
  197.6 12.8 %conditional.7 = ((f32[128,4,8,128]{3,0,2,1:T(8,128)S(1)}, bf16[2048,1024]{0,1:T(8,128)(2,1)})) conditional(s32[]{:T(128)} %convert_element_type.79, (f32[128,4,8,128]{3,0,2,1:T(8,128)S(1)}, bf16[2048,1024]{0,1:T(8,128)(2,1)}) %tuple.146, (pred[128,1,1,512]{0,3,2,1:T(8,128)(4,1)S(1)}, s32[]{:T(128)}, bf16[2048,512]{0,1:T(8,128)(2,1)}, ...), branch_computations={%region_17.17_spmd, %region_18.18_spmd} | conditional | flops 2712666112 | bytes 57327708 | solution.py:160
  197.6 1.3 constant_dynamic-slice_fusion.2
  198.9 1.3 fusion.48
  200.2 3.1 %fusion.21 = bf16[128,4,8,512]{0,3,2,1:T(8,128)(2,1)S(1)} fusion(f32[4,512,128,8]{2,1,3,0:T(8,128)S(1)} %fusion.48, f32[128,4,8]{0,2,1:T(8,128)S(1)} %get-tuple-element.695, f32[128,4,8]{0,2,1:T(8,128)S(1)} %get-tuple-element.692, pred[128,512]{0,1:T(8,128)(4,1)S(1)} %bitcast.131, bf16[512,4,128,1]{0,2,3,1:T(8,128)(2,1)S(1)} %bitcast.126, ...), kind=kOutput, calls=%fused_computation.35 | convolution fusion | flops 551550976 | bytes 14254080 | tf_op jit(solution)/shard_map/while/body/eval_jaxpr/cond/branch_1_fun/rgjd,ngd->rgjn/dot_general | solution.py:134
  203.3 1.5 fusion.29
  204.8 2.2 fusion.26
  208.1 2.3 bitcast_add_fusion.1
  210.5 6.4 %copy.115 = bf16[2048,1024]{1,0:T(8,128)(2,1)} copy(bf16[2048,1024]{0,1:T(8,128)(2,1)} %get-tuple-element.724) | data formatting | bytes 8388608 | tf_op jit(solution)/shard_map/while | solution.py:166
  216.9 1.2 copy-done.1
  218.1 1.3 copy.145
  221.6 1.3 broadcast_in_dim_reshape.3
  222.9 31.9 %collective-permute-done = bf16[128,4096]{1,0:T(8,128)(2,1)} collective-permute-done((bf16[128,4096]{1,0:T(8,128)(2,1)}, bf16[128,4096]{1,0:T(8,128)(2,1)}, u32[]{:S(2)}, u32[]{:S(2)}) %collective-permute-start) | collective-permute-done | bytes 1048608 | tf_op jit(solution)/shard_map/ppermute | solution.py:20
  254.8 33.3 %reduce-scatter.2.cloned.1.call-done = bf16[128,1024]{1,0:T(8,128)(2,1)} async-done(((bf16[2048,1024]{1,0:T(8,128)(2,1)}), bf16[128,1024]{1,0:T(8,128)(2,1)}) %reduce-scatter.2.cloned.1.call-update) | async-done | bytes 262160 | tf_op jit(solution)/shard_map/reduce_scatter | solution.py:167
  289.9 2.3 copy.175
  (74 shorter events, 20.8 us)
Async XLA Ops:
  7.2 44.1 %all-gather.5.cloned.1.call-start = ((), (), s32[]{:S(2)}) async-start(), calls=%async_computation.2 | async-start | bytes 2228224 | tf_op jit(solution)/shard_map/all_gather | solution.py:79
  8.9 97.4 %all-gather.7.cloned.1.call-start = ((), (), s32[]{:S(2)}) async-start(), calls=%async_computation.3 | async-start | bytes 2228224 | tf_op jit(solution)/shard_map/all_gather | solution.py:80
  10.6 277.4 %reduce-scatter.2.cloned.1.call-start = ((), (), s32[]{:S(2)}) async-start(), calls=%async_computation.1 | async-start | bytes 4456448 | tf_op jit(solution)/shard_map/reduce_scatter | solution.py:167
  10.7 28.9 %collective-permute-start.1 = (bf16[128,4096]{1,0:T(8,128)(2,1)}, bf16[128,4096]{1,0:T(8,128)(2,1)}, u32[]{:S(2)}, u32[]{:S(2)}) collective-permute-start(bf16[128,4096]{1,0:T(8,128)(2,1)} %bitcast.134), channel_id=1, source_target_pairs={{1,0},{2,1},{3,2},{4,3},{5,4},{6,5},{7,6},{0,7},{9,8},{10,9},{11,1... | collective-permute-start | bytes 3145736 | tf_op jit(solution)/shard_map/ppermute | solution.py:20
  41.2 107.8 %copy-start.2 = (bf16[128,4096]{0,1:T(8,128)(2,1)}, bf16[128,4096]{0,1:T(8,128)(2,1)S(1)}, u32[]{:S(2)}) copy-start(bf16[128,4096]{0,1:T(8,128)(2,1)S(1)} %copy.113) | copy-start | bytes 3145732
  51.2 56.7 %copy-start.4 = (s32[32]{0:T(128)S(1)}, s32[32]{0:T(128)}, u32[]{:S(2)}) copy-start(s32[32]{0:T(128)} %param.19) | copy-start | bytes 388
  149.0 1.0 copy-start
  155.7 1.3 copy-start.3
  170.1 1.3 copy-start.3
  184.5 1.3 copy-start.3
  198.9 1.3 copy-start.3
  216.9 1.2 copy-start.1
  219.4 35.4 %collective-permute-start = (bf16[128,4096]{1,0:T(8,128)(2,1)}, bf16[128,4096]{1,0:T(8,128)(2,1)}, u32[]{:S(2)}, u32[]{:S(2)}) collective-permute-start(bf16[128,4096]{1,0:T(8,128)(2,1)} %copy.145), channel_id=1, source_target_pairs={{7,0},{0,1},{1,2},{2,3},{3,4},{4,5},{5,6},{6,7},{15,8},{8,9},{9,10... | collective-permute-start | bytes 3145736 | tf_op jit(solution)/shard_map/ppermute | solution.py:20
Sparse Core Ops, SparseCore 0:
  10.2 41.0 all-gather.4
  53.4 52.8 all-gather.6
  217.0 70.9 reduce-scatter.1
where the time goes:
time: 301 us; the launch traced here: 299 us
  waiting for transfers between devices  115 us (38%)
  matrix products  84.2 us (28%)
  local copies, waits for them, and re-layouts  38.8 us (13%)
  other arithmetic  31.9 us (11%)
  between operations  14.5 us (5%)
  starting transfers between devices  8 us (3%)
  loops' own time  5.97 us (2%)
    ppermute x2, waiting for transfers between devices, from_behind(): return lax.ppermute(block, axis, route)  48 us
    reduce_scatter x1, waiting for transfers between devices, body(): lax.psum_scatter(key_terms.astype(jnp.bfloat16), 'ctx', scatter_dimension...  33.3 us
    dot_general x4, matrix products, attend_update(): jnp.einsum('rgjn,ngd->rgjd', weights, value_heads, preferred_element_type...  27.8 us
    all_gather x1, waiting for transfers between devices, body(): lax.all_gather(value_local, 'ctx', axis=0, tiled=True)  23.9 us
    dot_general x1, matrix products, stats_update(): jnp.einsum('rgjd,ngd->rgjn', query_heads, key_heads, preferred_element_ty...  14.9 us
    reduce_sum x1, other arithmetic, stats_update(): denominator = jnp.sum(probabilities, axis=-1)  14.8 us
    dot_general x4, matrix products, backward_update(): jnp.einsum('rgjd,ngd->rgjn', grad_heads, value_heads, preferred_element_t...  12.4 us
    dynamic_slice x8, local copies, waits for them, and re-layouts, block_inputs(): lax.dynamic_slice_in_dim(all_values, first_row, block_rows, 0)  10.2 us
  transfers between devices with their start and end apart: 5, of which 5 were waited for; matrix products, arithmetic and copies ran while one was open for 15% of the time, Pallas kernels for 0%

commit v1 on v0

v1 whole, which is shorter than its diff:
```python
import functools
import math

import jax
import jax.numpy as jnp
from jax import lax
from jax.experimental import pallas as pl
from jax.experimental.pallas import tpu as pltpu
from jax.sharding import PartitionSpec as P

BLK = 64
HEADS = 32
KV_HEADS = 4
HEAD_DIM = 128
GROUP = HEADS // KV_HEADS
WIDE = GROUP * HEAD_DIM
ROWS = GROUP * BLK
CHUNK = 512
MASKED = -1e30
SCALE = 1.0 / math.sqrt(HEAD_DIM)
EXP2_SCALE = SCALE * math.log2(math.e)
VMEM_LIMIT = 56 * 2**20

f32 = jnp.float32
bf16 = jnp.bfloat16


def dot_nt(a, b):
    return lax.dot_general(a, b, (((1,), (1,)), ((), ())), preferred_element_type=f32)


def dot_nn(a, b):
    return lax.dot_general(a, b, (((1,), (0,)), ((), ())), preferred_element_type=f32)


def attention_kernel(
    which, slots, q_all, q_far, g_near, g_far, kv,
    o_near, o_far, dq_near, dq_far, dkv,
    q_near, ks, vs, kt, vt, st, eb, qs, gs, gt, dk_acc, dv_acc, m_ref, ot, dqt, sem,
):
    me = lax.axis_index("ctx")
    core = lax.rem(me, 2)
    col = pl.multiple_of((2 * core + which) * WIDE, WIDE)
    fetch = pltpu.make_async_copy(q_all.at[0, :, pl.ds(col, WIDE)], q_near, sem)
    fetch.start()
    blocks = kv.shape[0] // BLK
    tokens = kv.shape[0]

    for b in range(blocks):
        to = pl.multiple_of(slots[b] * BLK, BLK)
        ks[pl.ds(to, BLK), :] = kv[b * BLK : (b + 1) * BLK, 0:HEAD_DIM]
        vs[pl.ds(to, BLK), 0:HEAD_DIM] = kv[b * BLK : (b + 1) * BLK, HEAD_DIM : 2 * HEAD_DIM]
    lane = lax.broadcasted_iota(jnp.int32, (tokens, HEAD_DIM), 1)
    vs[:, HEAD_DIM : 2 * HEAD_DIM] = jnp.where(lane < 2, 1.0, 0.0).astype(bf16)
    for c in range(tokens // 256):
        part = slice(c * 256, (c + 1) * 256)
        kt[:, part] = ks[part, :].T
        vt[0:HEAD_DIM, part] = vs[part, 0:HEAD_DIM].T
    sub = lax.broadcasted_iota(jnp.int32, (16, tokens), 0)
    vt[HEAD_DIM : HEAD_DIM + 16, :] = jnp.where(sub == 0, 1.0, 0.0).astype(bf16)
    dk_acc[...] = jnp.zeros_like(dk_acc)
    dv_acc[...] = jnp.zeros_like(dv_acc)
    fetch.wait()

    for t in range(4):
        q, g, o, dq = (
            (q_near, g_near, o_near, dq_near) if t < 2 else (q_far, g_far, o_far, dq_far)
        )
        owner = me if t < 2 else me + 1 - 2 * core
        r0 = (t % 2) * BLK
        for h in range(GROUP):
            qs[h * BLK : (h + 1) * BLK, :] = q[r0 : r0 + BLK, h * HEAD_DIM : (h + 1) * HEAD_DIM]
            gs[h * BLK : (h + 1) * BLK, :] = g[r0 : r0 + BLK, h * HEAD_DIM : (h + 1) * HEAD_DIM]
        pos = slots[2 * owner + t % 2]
        last = (pos * BLK) // CHUNK
        qv = qs[...]

        def score(c, highest, masked):
            off = pl.multiple_of(c * CHUNK, CHUNK)
            s = dot_nt(ks[pl.ds(off, CHUNK), :], qv)
            if masked:
                key_pos = off + lax.broadcasted_iota(jnp.int32, (CHUNK, ROWS), 0)
                query_pos = pos * BLK + lax.broadcasted_iota(jnp.int32, (CHUNK, ROWS), 1) % BLK
                s = jnp.where(key_pos <= query_pos, s, MASKED)
            st[pl.ds(off, CHUNK), :] = s
            return jnp.maximum(highest, jnp.max(s.reshape(CHUNK // 8, 8, ROWS), axis=0))

        highest = lax.fori_loop(
            0, last, lambda c, m: score(c, m, False), jnp.full((8, ROWS), MASKED, f32)
        )
        highest = score(last, highest, True)
        m_ref[...] = jnp.max(highest, axis=0, keepdims=True)
        ot[...] = jnp.zeros_like(ot)

        def attend(c, _):
            off = pl.multiple_of(c * CHUNK, CHUNK)
            e = jnp.exp2((st[pl.ds(off, CHUNK), :] - m_ref[...]) * EXP2_SCALE).astype(bf16)
            eb[pl.ds(off, CHUNK), :] = e
            ot[...] += dot_nn(vt[:, pl.ds(off, CHUNK)], e)
            return 0

        lax.fori_loop(0, last + 1, attend, 0)
        inverse = 1.0 / ot[HEAD_DIM : HEAD_DIM + 1, :]
        attended_t = ot[0:HEAD_DIM, :] * inverse
        attended = attended_t.T.astype(bf16)
        for h in range(GROUP):
            o[r0 : r0 + BLK, h * HEAD_DIM : (h + 1) * HEAD_DIM] = attended[h * BLK : (h + 1) * BLK, :]
        scaled = (gs[...].T.astype(f32) * inverse).astype(bf16)
        gt[0:HEAD_DIM, :] = scaled
        gs[...] = scaled.T
        minus_delta = -jnp.sum(scaled.astype(f32) * attended_t, axis=0, keepdims=True)
        high = minus_delta.astype(bf16).astype(f32)
        low = minus_delta - high
        row = lax.broadcasted_iota(jnp.int32, (HEAD_DIM, ROWS), 0)
        gt[HEAD_DIM : 2 * HEAD_DIM, :] = jnp.where(
            row == 0, high, jnp.where(row == 1, low, 0.0)
        ).astype(bf16)
        dqt[...] = jnp.zeros_like(dqt)

        def backward(c, _):
            off = pl.multiple_of(c * CHUNK, CHUNK)
            centred = dot_nn(vs[pl.ds(off, CHUNK), :], gt[...])
            e = eb[pl.ds(off, CHUNK), :]
            ds = (e.astype(f32) * centred).astype(bf16)
            dv_acc[pl.ds(off, CHUNK), :] += dot_nn(e, gs[...])
            dk_acc[pl.ds(off, CHUNK), :] += dot_nn(ds, qs[...])
            dqt[...] += dot_nn(kt[:, pl.ds(off, CHUNK)], ds)
            return 0

        lax.fori_loop(0, last + 1, backward, 0)
        grad = (dqt[...] * SCALE).T.astype(bf16)
        for h in range(GROUP):
            dq[r0 : r0 + BLK, h * HEAD_DIM : (h + 1) * HEAD_DIM] = grad[h * BLK : (h + 1) * BLK, :]

    for b in range(blocks):
        at = pl.multiple_of(slots[b] * BLK, BLK)
        rows = slice(b * BLK, (b + 1) * BLK)
        dkv[rows, 0:HEAD_DIM] = (dk_acc[pl.ds(at, BLK), :] * SCALE).astype(bf16)
        dkv[rows, HEAD_DIM : 2 * HEAD_DIM] = dv_acc[pl.ds(at, BLK), :].astype(bf16)


def attention(which, slots, q_all, q_far, g_near, g_far, kv):
    local = q_far.shape[0]
    tokens = kv.shape[0]
    vmem = pl.BlockSpec(memory_space=pltpu.VMEM)
    piece = jax.ShapeDtypeStruct((local, WIDE), bf16)
    return pl.pallas_call(
        functools.partial(attention_kernel, which),
        out_shape=(piece,) * 4 + (jax.ShapeDtypeStruct((tokens, 2 * HEAD_DIM), bf16),),
        in_specs=[
            pl.BlockSpec(memory_space=pltpu.SMEM),
            pl.BlockSpec(memory_space=pl.ANY),
        ] + [vmem] * 4,
        out_specs=(vmem,) * 5,
        scratch_shapes=[
            pltpu.VMEM((local, WIDE), bf16),
            pltpu.VMEM((tokens, HEAD_DIM), bf16),
            pltpu.VMEM((tokens, 2 * HEAD_DIM), bf16),
            pltpu.VMEM((HEAD_DIM, tokens), bf16),
            pltpu.VMEM((HEAD_DIM + 16, tokens), bf16),
            pltpu.VMEM((tokens, ROWS), f32),
            pltpu.VMEM((tokens, ROWS), bf16),
            pltpu.VMEM((ROWS, HEAD_DIM), bf16),
            pltpu.VMEM((ROWS, HEAD_DIM), bf16),
            pltpu.VMEM((2 * HEAD_DIM, ROWS), bf16),
            pltpu.VMEM((tokens, HEAD_DIM), f32),
            pltpu.VMEM((tokens, HEAD_DIM), f32),
            pltpu.VMEM((1, ROWS), f32),
            pltpu.VMEM((HEAD_DIM + 16, ROWS), f32),
            pltpu.VMEM((HEAD_DIM, ROWS), f32),
            pltpu.SemaphoreType.DMA,
        ],
        compiler_params=pltpu.CompilerParams(vmem_limit_bytes=VMEM_LIMIT),
    )(slots, q_all, q_far, g_near, g_far, kv)


def join_kernel(near_a, far_a, near_b, far_b, out):
    core = lax.rem(lax.axis_index("ctx"), 2)
    for which, near, far in ((0, near_a, far_a), (1, near_b, far_b)):
        out[0, :, pl.ds(pl.multiple_of((2 * core + which) * WIDE, WIDE), WIDE)] = near[...]
        out[0, :, pl.ds(pl.multiple_of((2 - 2 * core + which) * WIDE, WIDE), WIDE)] = far[...]


def join(*pieces):
    vmem = pl.BlockSpec(memory_space=pltpu.VMEM)
    return pl.pallas_call(
        join_kernel,
        out_shape=jax.ShapeDtypeStruct((1, pieces[0].shape[0], HEADS * HEAD_DIM), bf16),
        in_specs=[vmem] * 4,
        out_specs=vmem,
        compiler_params=pltpu.CompilerParams(vmem_limit_bytes=VMEM_LIMIT),
    )(*pieces)


def total_kernel(local, part_a, part_b, dk, dv):
    sources = part_a.shape[0] // local
    for core in range(2):
        for which, part in ((0, part_a), (1, part_b)):
            total = jnp.zeros((local, 2 * HEAD_DIM), f32)
            for s in range(core, sources, 2):
                total = total + part[s * local : (s + 1) * local, :].astype(f32)
            head = 2 * core + which
            columns = slice(head * HEAD_DIM, (head + 1) * HEAD_DIM)
            dk[0, :, columns] = total[:, 0:HEAD_DIM]
            dv[0, :, columns] = total[:, HEAD_DIM : 2 * HEAD_DIM]


def totals(local, part_a, part_b):
    vmem = pl.BlockSpec(memory_space=pltpu.VMEM)
    return pl.pallas_call(
        functools.partial(total_kernel, local),
        out_shape=(jax.ShapeDtypeStruct((1, local, KV_HEADS * HEAD_DIM), f32),) * 2,
        in_specs=[vmem] * 2,
        out_specs=(vmem,) * 2,
        compiler_params=pltpu.CompilerParams(vmem_limit_bytes=VMEM_LIMIT),
    )(part_a, part_b)


def pair_swap(x):
    n = lax.axis_size("ctx")
    return lax.ppermute(x, "ctx", [(i, i ^ 1) for i in range(n)])


def to_section(x, step, swap):
    n, sections = lax.axis_size("ctx"), lax.axis_size("section")
    route = [
        (i * sections + s, (i ^ swap) * sections + (s + step) % sections)
        for i in range(n)
        for s in range(sections)
    ]
    return lax.ppermute(x, ("ctx", "section"), route)


def exchange(x):
    return lax.all_to_all(x, "ctx", 0, 0, tiled=True)


def body(queries, key_vectors, value_vectors, cotangent, slot_order):
    members = lax.axis_size("ctx")
    core = lax.rem(lax.axis_index("ctx"), 2)
    local = queries.shape[1]
    near = [2 * core + which for which in range(2)]
    far = [2 - 2 * core + which for which in range(2)]

    def part(x, head):
        return lax.dynamic_slice_in_dim(x[0], head * WIDE, WIDE, 1)

    def packed(which):
        halves = []
        for head in (which, 2 + which):
            columns = slice(head * HEAD_DIM, (head + 1) * HEAD_DIM)
            halves += [key_vectors[0][:, columns], value_vectors[0][:, columns]]
        two = jnp.stack(
            [jnp.concatenate(halves[0:2], axis=1), jnp.concatenate(halves[2:4], axis=1)]
        )
        return jnp.broadcast_to(two[None], (members // 2,) + two.shape).reshape(
            members * local, 2 * HEAD_DIM
        )

    kv = [exchange(packed(which)) for which in range(2)]
    q_far = [pair_swap(part(queries, far[which])) for which in range(2)]
    g_near = [to_section(part(cotangent, near[which]), -1, 0) for which in range(2)]
    g_far = [to_section(part(cotangent, far[which]), -1, 1) for which in range(2)]
    o_near, o_far, dq_near, dq_far, partial = [], [], [], [], []
    for which in range(2):
        a, b, c, d, e = attention(
            which, slot_order, queries, q_far[which], g_near[which], g_far[which], kv[which]
        )
        o_near.append(to_section(a, 1, 0))
        o_far.append(to_section(b, 1, 1))
        dq_near.append(c)
        dq_far.append(pair_swap(d))
        partial.append(exchange(e))
    handed = join(o_near[0], o_far[0], o_near[1], o_far[1])
    grad_query = join(dq_near[0], dq_far[0], dq_near[1], dq_far[1])
    grad_key, grad_value = totals(local, *partial)
    return handed, grad_query, grad_key, grad_value


def solution(mesh):
    tokens = P("section", "ctx", None)
    return jax.shard_map(
        body,
        mesh=mesh,
        in_specs=(tokens,) * 4 + (P(),),
        out_specs=(tokens,) * 4,
        check_vma=False,
    )
```

time: 301 us -> 184 us (0.61); the launches traced: 299 us -> 185 us
  matrix products: 84.2 us -> 0 us
  starting transfers between devices: 8 us -> 52.3 us
  Pallas kernels: 0 us -> 43.2 us
  waiting for transfers between devices: 115 us -> 78.5 us
  other arithmetic: 31.9 us -> 0.07 us
  local copies, waits for them, and re-layouts: 38.8 us -> 10.3 us
  between operations: 14.5 us -> 0.88 us
  loops' own time: 5.97 us -> 0 us
    dot_general x25 -> x0, matrix products: 84.2 us -> none  [the longest x4 27.8 us: attend_update(): jnp.einsum('rgjn,ngd->rgjd', weights, value_heads, preferred_element_type...]
    pallas_call x0 -> x5, Pallas kernels: none -> 43.2 us  [the longest x2 36.2 us: attention(): pl.pallas_call(functools.partial(attention_kernel, which), out_shape=(pie...]
    all_gather x2 -> x0, waiting for transfers between devices: 34 us -> none  [the longest x1 23.9 us: body(): lax.all_gather(value_local, 'ctx', axis=0, tiled=True)]
    reduce_scatter x1 -> x0, waiting for transfers between devices: 33.3 us -> none  [body(): lax.psum_scatter(key_terms.astype(jnp.bfloat16), 'ctx', scatter_dimension...]
    all_to_all x0 -> x4, starting transfers between devices: none -> 31.5 us  [exchange(): return lax.all_to_all(x, 'ctx', 0, 0, tiled=True)]
    reduce_sum x12 -> x0, other arithmetic: 17.5 us -> none  [the longest x1 14.8 us: stats_update(): denominator = jnp.sum(probabilities, axis=-1)]
    all_to_all x0 -> x4, waiting for transfers between devices: none -> 15.8 us  [exchange(): return lax.all_to_all(x, 'ctx', 0, 0, tiled=True)]
    ppermute x2 -> x12, waiting for transfers between devices: 48 us -> 62.7 us  [the longest x8 62.7 us: to_section(): return lax.ppermute(x, ('ctx', 'section'), route)]
  transfers between devices with their start and end apart: 5 -> 16, of which waited for: 5 -> 9; matrix products, arithmetic and copies ran while one was open for 15% -> 0% of each run, Pallas kernels for 0% -> 22%
where the time goes in v1:
time: 184 us; the launch traced here: 185 us
  waiting for transfers between devices  78.5 us (43%)
  starting transfers between devices  52.3 us (28%)
  Pallas kernels  43.2 us (23%)
  local copies, waits for them, and re-layouts  10.3 us (6%)
    ppermute x8, waiting for transfers between devices, to_section(): return lax.ppermute(x, ('ctx', 'section'), route)  62.7 us
    pallas_call x2, Pallas kernels, attention(): pl.pallas_call(functools.partial(attention_kernel, which), out_shape=(pie...  36.2 us
    all_to_all x4, starting transfers between devices, exchange(): return lax.all_to_all(x, 'ctx', 0, 0, tiled=True)  31.5 us
    ppermute x8, starting transfers between devices, to_section(): return lax.ppermute(x, ('ctx', 'section'), route)  18.6 us
    all_to_all x4, waiting for transfers between devices, exchange(): return lax.all_to_all(x, 'ctx', 0, 0, tiled=True)  15.8 us
    unnamed x48, local copies, waits for them, and re-layouts  6.27 us
    pallas_call x2, Pallas kernels, join(): pl.pallas_call(join_kernel, out_shape=jax.ShapeDtypeStruct((1, pieces[0]....  4.47 us
  transfers between devices with their start and end apart: 16, of which 9 were waited for; matrix products, arithmetic and copies ran while one was open for 0% of the time, Pallas kernels for 22%

profile of v1, /device:TPU:1, one launch (start us, length us, event | category | flops | bytes accessed | tf_op | source)
XLA Modules:
  0.0 185.3 jit_solution(8710324435743345043)
XLA Ops:
  0.6 0.0 copy-start.18
  0.6 0.9 fusion
  1.5 0.1 copy-done.18
  1.7 1.1 broadcast_in_dim.4
  2.8 7.3 %all-to-all-start = ((bf16[16,128,256]{2,1,0:T(8,128)(2,1)}), bf16[16,128,256]{2,1,0:T(8,128)(2,1)S(1)}, u32[]{:S(2)}, u32[]{:S(2)}) async-start(bf16[16,128,256]{2,1,0:T(8,128)(2,1)} %bitcast.7), calls=%async_computation | async-start | bytes 2097152 | tf_op jit(solution)/shard_map/all_to_all | solution.py:235
  10.1 15.8 %all-to-all-done = bf16[16,128,256]{2,1,0:T(8,128)(2,1)S(1)} async-done(((bf16[16,128,256]{2,1,0:T(8,128)(2,1)}), bf16[16,128,256]{2,1,0:T(8,128)(2,1)S(1)}, u32[]{:S(2)}, u32[]{:S(2)}) %all-to-all-start) | async-done | bytes 1048608 | tf_op jit(solution)/shard_map/all_to_all | solution.py:235
  25.9 1.3 broadcast_in_dim.5
  27.2 0.0 copy-done.2
  27.3 4.3 %all-to-all-start.1 = ((bf16[16,128,256]{2,1,0:T(8,128)(2,1)}), bf16[16,128,256]{2,1,0:T(8,128)(2,1)S(1)}, u32[]{:S(2)}, u32[]{:S(2)}) async-start(bf16[16,128,256]{2,1,0:T(8,128)(2,1)} %bitcast.33), calls=%async_computation.1 | async-start | bytes 2097152 | tf_op jit(solution)/shard_map/all_to_all | solution.py:235
  31.6 0.0 copy-done
  31.6 0.7 dynamic-slice_bitcast_fusion.2
  32.3 0.2 collective-permute-start
  32.6 0.3 copy-done.5
  32.9 0.1 dynamic-slice_bitcast_fusion
  33.0 5.7 %collective-permute-start.2 = (bf16[128,1024]{1,0:T(8,128)(2,1)S(1)}, bf16[128,1024]{1,0:T(8,128)(2,1)S(1)}, u32[]{:S(2)}, u32[]{:S(2)}) collective-permute-start(bf16[128,1024]{1,0:T(8,128)(2,1)S(1)} %get-tuple-element.29), channel_id=1, source_target_pairs={{0,15},{1,8},{2,9},{3,10},{4,11},{5,12},{6,13},{7,14},{8,7},{9,0},... | collective-permute-start | bytes 786440 | tf_op jit(solution)/shard_map/ppermute | solution.py:231
  38.6 0.5 collective-permute-start.1
  39.2 0.0 collective-permute-done.q_far
  39.2 8.7 %collective-permute-done.2.g_far = bf16[128,1024]{1,0:T(8,128)(2,1)S(1)} collective-permute-done((bf16[128,1024]{1,0:T(8,128)(2,1)S(1)}, bf16[128,1024]{1,0:T(8,128)(2,1)S(1)}, u32[]{:S(2)}, u32[]{:S(2)}) %collective-permute-start.2) | collective-permute-done | bytes 262176 | tf_op jit(solution)/shard_map/ppermute | solution.py:231
  47.9 7.2 %collective-permute-done.1.g_near = bf16[128,1024]{1,0:T(8,128)(2,1)S(1)} collective-permute-done((bf16[128,1024]{1,0:T(8,128)(2,1)S(1)}, bf16[128,1024]{1,0:T(8,128)(2,1)S(1)}, u32[]{:S(2)}, u32[]{:S(2)}) %collective-permute-start.1) | collective-permute-done | bytes 262176 | tf_op jit(solution)/shard_map/ppermute | solution.py:231
  55.1 0.7 copy-done.10
  55.8 17.9 %shard_map.84 = (bf16[128,1024]{1,0:T(8,128)(2,1)}, bf16[128,1024]{1,0:T(8,128)(2,1)}, bf16[128,1024]{1,0:T(8,128)(2,1)}, bf16[128,1024]{1,0:T(8,128)(2,1)}, bf16[2048,256]{1,0:T(8,128)(2,1)}) custom-call(s32[32]{0:T(128)} %slots.3, bf16[1,128,4096]{2,1,0:T(8,128)(2,1)} %q_all.3, bf16[128,1024]{1,0:T(8,128)(2,1)} %copy-done.6, bf16[128,1024]{1,0:T(8,128)(2,1)} %copy-done.10, ...), custom_call_target="tpu_custom_call" | custom-call | tf_op jit(solution)/shard_map/pallas_call | solution.py:147
  73.7 0.0 all-to-all-done.1
  73.7 0.0 copy-start.1
  73.7 1.0 copy-done.1
  74.7 9.9 %all-to-all-start.2 = ((bf16[16,128,256]{2,1,0:T(8,128)(2,1)}), bf16[16,128,256]{2,1,0:T(8,128)(2,1)S(1)}, u32[]{:S(2)}, u32[]{:S(2)}) async-start(bf16[16,128,256]{2,1,0:T(8,128)(2,1)} %bitcast.36), calls=%async_computation.2 | async-start | bytes 2097152 | tf_op jit(solution)/shard_map/all_to_all | solution.py:235
  84.6 0.2 collective-permute-start.5
  84.8 6.7 %collective-permute-start.7 = (bf16[128,1024]{1,0:T(8,128)(2,1)S(1)}, bf16[128,1024]{1,0:T(8,128)(2,1)S(1)}, u32[]{:S(2)}, u32[]{:S(2)}) collective-permute-start(bf16[128,1024]{1,0:T(8,128)(2,1)S(1)} %get-tuple-element.28), channel_id=1, source_target_pairs={{0,15},{1,8},{2,9},{3,10},{4,11},{5,12},{6,13},{7,14},{8,7},{9,0},... | collective-permute-start | bytes 786440 | tf_op jit(solution)/shard_map/ppermute | solution.py:231
  91.4 0.0 collective-permute-start.6
  91.5 0.0 collective-permute-done.5.q_far
  91.5 9.1 %collective-permute-done.7.g_far = bf16[128,1024]{1,0:T(8,128)(2,1)S(1)} collective-permute-done((bf16[128,1024]{1,0:T(8,128)(2,1)S(1)}, bf16[128,1024]{1,0:T(8,128)(2,1)S(1)}, u32[]{:S(2)}, u32[]{:S(2)}) %collective-permute-start.7) | collective-permute-done | bytes 262176 | tf_op jit(solution)/shard_map/ppermute | solution.py:231
  100.6 9.2 %collective-permute-done.6.g_near = bf16[128,1024]{1,0:T(8,128)(2,1)S(1)} collective-permute-done((bf16[128,1024]{1,0:T(8,128)(2,1)S(1)}, bf16[128,1024]{1,0:T(8,128)(2,1)S(1)}, u32[]{:S(2)}, u32[]{:S(2)}) %collective-permute-start.6) | collective-permute-done | bytes 262176 | tf_op jit(solution)/shard_map/ppermute | solution.py:231
  109.8 0.7 copy-done.11
  110.5 18.2 %shard_map.85 = (bf16[128,1024]{1,0:T(8,128)(2,1)}, bf16[128,1024]{1,0:T(8,128)(2,1)}, bf16[128,1024]{1,0:T(8,128)(2,1)}, bf16[128,1024]{1,0:T(8,128)(2,1)}, bf16[2048,256]{1,0:T(8,128)(2,1)}) custom-call(s32[32]{0:T(128)} %slots.3, bf16[1,128,4096]{2,1,0:T(8,128)(2,1)} %q_all.3, bf16[128,1024]{1,0:T(8,128)(2,1)} %copy-done.7, bf16[128,1024]{1,0:T(8,128)(2,1)} %copy-done.11, ...), custom_call_target="tpu_custom_call" | custom-call | tf_op jit(solution)/shard_map/pallas_call | solution.py:147
  128.7 0.0 all-to-all-done.2
  128.7 0.0 copy-start.3
  128.7 0.0 copy-start.21
  128.8 0.0 copy-start.20
  128.8 0.0 copy-start.19
  128.8 0.0 copy-start.23
  128.8 0.0 copy-start.22
  128.8 0.9 copy-done.3
  129.7 10.0 %all-to-all-start.3 = ((bf16[16,128,256]{2,1,0:T(8,128)(2,1)}), bf16[16,128,256]{2,1,0:T(8,128)(2,1)S(1)}, u32[]{:S(2)}, u32[]{:S(2)}) async-start(bf16[16,128,256]{2,1,0:T(8,128)(2,1)} %bitcast.35), calls=%async_computation.3 | async-start | bytes 2097152 | tf_op jit(solution)/shard_map/all_to_all | solution.py:235
  139.7 0.1 collective-permute-start.3
  139.8 0.1 collective-permute-start.4
  139.9 0.2 collective-permute-start.10
  140.1 5.2 %collective-permute-start.8 = (bf16[128,1024]{1,0:T(8,128)(2,1)}, bf16[128,1024]{1,0:T(8,128)(2,1)S(1)}, u32[]{:S(2)}, u32[]{:S(2)}) collective-permute-start(bf16[128,1024]{1,0:T(8,128)(2,1)} %get-tuple-element.18), channel_id=1, source_target_pairs={{0,1},{1,2},{2,3},{3,4},{4,5},{5,6},{6,7},{7,0},{8,9},{9,10},{10,1... | collective-permute-start | bytes 786440 | tf_op jit(solution)/shard_map/ppermute | solution.py:231
  145.3 0.4 collective-permute-start.9
  145.6 12.6 %collective-permute-done.3.near_a = bf16[128,1024]{1,0:T(8,128)(2,1)S(1)} collective-permute-done((bf16[128,1024]{1,0:T(8,128)(2,1)S(1)}, bf16[128,1024]{1,0:T(8,128)(2,1)S(1)}, u32[]{:S(2)}, u32[]{:S(2)}) %collective-permute-start.3) | collective-permute-done | bytes 262176 | tf_op jit(solution)/shard_map/ppermute | solution.py:231
  158.2 1.7 collective-permute-start.11
  159.9 4.9 %collective-permute-done.4.far_a = bf16[128,1024]{1,0:T(8,128)(2,1)S(1)} collective-permute-done((bf16[128,1024]{1,0:T(8,128)(2,1)S(1)}, bf16[128,1024]{1,0:T(8,128)(2,1)S(1)}, u32[]{:S(2)}, u32[]{:S(2)}) %collective-permute-start.4) | collective-permute-done | bytes 262176 | tf_op jit(solution)/shard_map/ppermute | solution.py:231
  164.8 5.3 %collective-permute-done.8.near_b = bf16[128,1024]{1,0:T(8,128)(2,1)S(1)} collective-permute-done((bf16[128,1024]{1,0:T(8,128)(2,1)}, bf16[128,1024]{1,0:T(8,128)(2,1)S(1)}, u32[]{:S(2)}, u32[]{:S(2)}) %collective-permute-start.8) | collective-permute-done | bytes 262176 | tf_op jit(solution)/shard_map/ppermute | solution.py:231
  170.1 5.7 %collective-permute-done.9.far_b = bf16[128,1024]{1,0:T(8,128)(2,1)S(1)} collective-permute-done((bf16[128,1024]{1,0:T(8,128)(2,1)S(1)}, bf16[128,1024]{1,0:T(8,128)(2,1)S(1)}, u32[]{:S(2)}, u32[]{:S(2)}) %collective-permute-start.9) | collective-permute-done | bytes 262176 | tf_op jit(solution)/shard_map/ppermute | solution.py:231
  175.8 0.0 copy-done.13
  175.8 0.7 copy-done.17
  176.5 2.2 %shard_map.86 = bf16[1,128,4096]{2,1,0:T(8,128)(2,1)} custom-call(bf16[128,1024]{1,0:T(8,128)(2,1)} %copy-done.13, bf16[128,1024]{1,0:T(8,128)(2,1)} %copy-done.14, bf16[128,1024]{1,0:T(8,128)(2,1)} %copy-done.16, bf16[128,1024]{1,0:T(8,128)(2,1)} %copy-done.17), custom_call_target="tpu_custom_call" | custom-call | tf_op jit(solution)/shard_map/pallas_call | solution.py:186
  178.7 0.0 collective-permute-done.10.far_a
  178.7 0.0 collective-permute-done.11.far_b
  178.7 0.0 copy-start.15
  178.8 0.7 copy-done.12
  179.4 0.1 copy-done.15
  179.5 2.2 %shard_map.87 = bf16[1,128,4096]{2,1,0:T(8,128)(2,1)} custom-call(bf16[128,1024]{1,0:T(8,128)(2,1)} %get-tuple-element.20.near_a, bf16[128,1024]{1,0:T(8,128)(2,1)} %copy-done.12, bf16[128,1024]{1,0:T(8,128)(2,1)} %get-tuple-element.22.near_b, bf16[128,1024]{1,0:T(8,128)(2,1)} %copy-done.15), custom_call_target="tpu_custom_call" | custom-call | tf_op jit(solution)/shard_map/pallas_call | solution.py:186
  181.8 0.0 all-to-all-done.3
  181.8 1.0 copy-done.4
  182.8 2.6 %shard_map.88 = (f32[1,128,512]{2,1,0:T(8,128)}, f32[1,128,512]{2,1,0:T(8,128)}) custom-call(bf16[2048,256]{1,0:T(8,128)(2,1)} %bitcast.32, bf16[2048,256]{1,0:T(8,128)(2,1)} %bitcast.34), custom_call_target="tpu_custom_call" | custom-call | tf_op jit(solution)/shard_map/pallas_call | solution.py:210
  (31 shorter events, 0.1 us)
Async XLA Ops:
  0.6 1.0 copy-start.18
  2.8 23.2 %all-to-all-start = ((bf16[16,128,256]{2,1,0:T(8,128)(2,1)}), bf16[16,128,256]{2,1,0:T(8,128)(2,1)S(1)}, u32[]{:S(2)}, u32[]{:S(2)}) async-start(bf16[16,128,256]{2,1,0:T(8,128)(2,1)} %bitcast.7), calls=%async_computation | async-start | bytes 2097152 | tf_op jit(solution)/shard_map/all_to_all | solution.py:235
  25.9 1.3 copy-start.2
  27.2 4.4 %copy-start = (bf16[1,128,4096]{2,1,0:T(8,128)(2,1)S(1)}, bf16[1,128,4096]{2,1,0:T(8,128)(2,1)}, u32[]{:S(2)}) copy-start(bf16[1,128,4096]{2,1,0:T(8,128)(2,1)} %q_all.3) | copy-start | bytes 3145732
  27.3 46.5 %all-to-all-start.1 = ((bf16[16,128,256]{2,1,0:T(8,128)(2,1)}), bf16[16,128,256]{2,1,0:T(8,128)(2,1)S(1)}, u32[]{:S(2)}, u32[]{:S(2)}) async-start(bf16[16,128,256]{2,1,0:T(8,128)(2,1)} %bitcast.33), calls=%async_computation.1 | async-start | bytes 2097152 | tf_op jit(solution)/shard_map/all_to_all | solution.py:235
  31.6 1.3 copy-start.5
  32.3 6.9 %collective-permute-start = (bf16[128,1024]{1,0:T(8,128)(2,1)}, bf16[128,1024]{1,0:T(8,128)(2,1)S(1)}, u32[]{:S(2)}, u32[]{:S(2)}) collective-permute-start(bf16[128,1024]{1,0:T(8,128)(2,1)} %get-tuple-element.33), channel_id=1, source_target_pairs={{0,8},{8,0},{16,24},{24,16},{32,40},{40,32},{48,56},{56,48},{64,72... | collective-permute-start | bytes 786440 | tf_op jit(solution)/shard_map/ppermute | solution.py:221
  33.0 14.9 %collective-permute-start.2 = (bf16[128,1024]{1,0:T(8,128)(2,1)S(1)}, bf16[128,1024]{1,0:T(8,128)(2,1)S(1)}, u32[]{:S(2)}, u32[]{:S(2)}) collective-permute-start(bf16[128,1024]{1,0:T(8,128)(2,1)S(1)} %get-tuple-element.29), channel_id=1, source_target_pairs={{0,15},{1,8},{2,9},{3,10},{4,11},{5,12},{6,13},{7,14},{8,7},{9,0},... | collective-permute-start | bytes 786440 | tf_op jit(solution)/shard_map/ppermute | solution.py:231
  38.6 16.4 %collective-permute-start.1 = (bf16[128,1024]{1,0:T(8,128)(2,1)S(1)}, bf16[128,1024]{1,0:T(8,128)(2,1)S(1)}, u32[]{:S(2)}, u32[]{:S(2)}) collective-permute-start(bf16[128,1024]{1,0:T(8,128)(2,1)S(1)} %get-tuple-element.30), channel_id=1, source_target_pairs={{0,7},{1,0},{2,1},{3,2},{4,3},{5,4},{6,5},{7,6},{8,15},{9,8},{10,9... | collective-permute-start | bytes 786440 | tf_op jit(solution)/shard_map/ppermute | solution.py:231
  39.2 15.9 %copy-start.6 = (bf16[128,1024]{1,0:T(8,128)(2,1)}, bf16[128,1024]{1,0:T(8,128)(2,1)S(1)}, u32[]{:S(2)}) copy-start(bf16[128,1024]{1,0:T(8,128)(2,1)S(1)} %collective-permute-done.q_far) | copy-start | bytes 786436
  47.9 7.2 %copy-start.9 = (bf16[128,1024]{1,0:T(8,128)(2,1)}, bf16[128,1024]{1,0:T(8,128)(2,1)S(1)}, u32[]{:S(2)}) copy-start(bf16[128,1024]{1,0:T(8,128)(2,1)S(1)} %collective-permute-done.2.g_far) | copy-start | bytes 786436
  55.1 0.7 copy-start.10
  73.7 1.0 copy-start.1
  74.7 54.0 %all-to-all-start.2 = ((bf16[16,128,256]{2,1,0:T(8,128)(2,1)}), bf16[16,128,256]{2,1,0:T(8,128)(2,1)S(1)}, u32[]{:S(2)}, u32[]{:S(2)}) async-start(bf16[16,128,256]{2,1,0:T(8,128)(2,1)} %bitcast.36), calls=%async_computation.2 | async-start | bytes 2097152 | tf_op jit(solution)/shard_map/all_to_all | solution.py:235
  84.6 6.9 %collective-permute-start.5 = (bf16[128,1024]{1,0:T(8,128)(2,1)S(1)}, bf16[128,1024]{1,0:T(8,128)(2,1)S(1)}, u32[]{:S(2)}, u32[]{:S(2)}) collective-permute-start(bf16[128,1024]{1,0:T(8,128)(2,1)S(1)} %get-tuple-element.32), channel_id=1, source_target_pairs={{0,8},{8,0},{16,24},{24,16},{32,40},{40,32},{48,56},{56,48},{64,72... | collective-permute-start | bytes 786440 | tf_op jit(solution)/shard_map/ppermute | solution.py:221
  84.8 15.8 %collective-permute-start.7 = (bf16[128,1024]{1,0:T(8,128)(2,1)S(1)}, bf16[128,1024]{1,0:T(8,128)(2,1)S(1)}, u32[]{:S(2)}, u32[]{:S(2)}) collective-permute-start(bf16[128,1024]{1,0:T(8,128)(2,1)S(1)} %get-tuple-element.28), channel_id=1, source_target_pairs={{0,15},{1,8},{2,9},{3,10},{4,11},{5,12},{6,13},{7,14},{8,7},{9,0},... | collective-permute-start | bytes 786440 | tf_op jit(solution)/shard_map/ppermute | solution.py:231
  91.4 18.4 %collective-permute-start.6 = (bf16[128,1024]{1,0:T(8,128)(2,1)S(1)}, bf16[128,1024]{1,0:T(8,128)(2,1)S(1)}, u32[]{:S(2)}, u32[]{:S(2)}) collective-permute-start(bf16[128,1024]{1,0:T(8,128)(2,1)S(1)} %get-tuple-element.31), channel_id=1, source_target_pairs={{0,7},{1,0},{2,1},{3,2},{4,3},{5,4},{6,5},{7,6},{8,15},{9,8},{10,9... | collective-permute-start | bytes 786440 | tf_op jit(solution)/shard_map/ppermute | solution.py:231
  91.5 18.4 %copy-start.7 = (bf16[128,1024]{1,0:T(8,128)(2,1)}, bf16[128,1024]{1,0:T(8,128)(2,1)S(1)}, u32[]{:S(2)}) copy-start(bf16[128,1024]{1,0:T(8,128)(2,1)S(1)} %collective-permute-done.5.q_far) | copy-start | bytes 786436
  100.6 9.2 %copy-start.8 = (bf16[128,1024]{1,0:T(8,128)(2,1)}, bf16[128,1024]{1,0:T(8,128)(2,1)S(1)}, u32[]{:S(2)}) copy-start(bf16[128,1024]{1,0:T(8,128)(2,1)S(1)} %collective-permute-done.7.g_far) | copy-start | bytes 786436
  109.8 0.7 copy-start.11
  128.7 1.0 copy-start.3
  128.7 11.0 %copy-start.21 = (bf16[128,1024]{1,0:T(8,128)(2,1)S(1)}, bf16[128,1024]{1,0:T(8,128)(2,1)}, u32[]{:S(2)}) copy-start(bf16[128,1024]{1,0:T(8,128)(2,1)} %get-tuple-element.16) | copy-start | bytes 786436
  128.8 11.0 %copy-start.20 = (bf16[128,1024]{1,0:T(8,128)(2,1)S(1)}, bf16[128,1024]{1,0:T(8,128)(2,1)}, u32[]{:S(2)}) copy-start(bf16[128,1024]{1,0:T(8,128)(2,1)} %get-tuple-element.17) | copy-start | bytes 786436
  128.8 11.1 %copy-start.19 = (bf16[128,1024]{1,0:T(8,128)(2,1)S(1)}, bf16[128,1024]{1,0:T(8,128)(2,1)}, u32[]{:S(2)}) copy-start(bf16[128,1024]{1,0:T(8,128)(2,1)} %get-tuple-element.21) | copy-start | bytes 786436
  128.8 16.5 %copy-start.23 = (bf16[128,1024]{1,0:T(8,128)(2,1)S(1)}, bf16[128,1024]{1,0:T(8,128)(2,1)}, u32[]{:S(2)}) copy-start(bf16[128,1024]{1,0:T(8,128)(2,1)} %get-tuple-element.19) | copy-start | bytes 786436
  128.8 29.5 %copy-start.22 = (bf16[128,1024]{1,0:T(8,128)(2,1)S(1)}, bf16[128,1024]{1,0:T(8,128)(2,1)}, u32[]{:S(2)}) copy-start(bf16[128,1024]{1,0:T(8,128)(2,1)} %get-tuple-element.23) | copy-start | bytes 786436
  129.7 52.0 %all-to-all-start.3 = ((bf16[16,128,256]{2,1,0:T(8,128)(2,1)}), bf16[16,128,256]{2,1,0:T(8,128)(2,1)S(1)}, u32[]{:S(2)}, u32[]{:S(2)}) async-start(bf16[16,128,256]{2,1,0:T(8,128)(2,1)} %bitcast.35), calls=%async_computation.3 | async-start | bytes 2097152 | tf_op jit(solution)/shard_map/all_to_all | solution.py:235
  139.7 18.5 %collective-permute-start.3 = (bf16[128,1024]{1,0:T(8,128)(2,1)S(1)}, bf16[128,1024]{1,0:T(8,128)(2,1)S(1)}, u32[]{:S(2)}, u32[]{:S(2)}) collective-permute-start(bf16[128,1024]{1,0:T(8,128)(2,1)S(1)} %copy-done.21), channel_id=1, source_target_pairs={{0,1},{1,2},{2,3},{3,4},{4,5},{5,6},{6,7},{7,0},{8,9},{9,10},{10,1... | collective-permute-start | bytes 786440 | tf_op jit(solution)/shard_map/ppermute | solution.py:231
  139.8 25.0 %collective-permute-start.4 = (bf16[128,1024]{1,0:T(8,128)(2,1)S(1)}, bf16[128,1024]{1,0:T(8,128)(2,1)S(1)}, u32[]{:S(2)}, u32[]{:S(2)}) collective-permute-start(bf16[128,1024]{1,0:T(8,128)(2,1)S(1)} %copy-done.20), channel_id=1, source_target_pairs={{0,9},{1,10},{2,11},{3,12},{4,13},{5,14},{6,15},{7,8},{8,1},{9,2},... | collective-permute-start | bytes 786440 | tf_op jit(solution)/shard_map/ppermute | solution.py:231
  139.9 38.9 %collective-permute-start.10 = (bf16[128,1024]{1,0:T(8,128)(2,1)S(1)}, bf16[128,1024]{1,0:T(8,128)(2,1)S(1)}, u32[]{:S(2)}, u32[]{:S(2)}) collective-permute-start(bf16[128,1024]{1,0:T(8,128)(2,1)S(1)} %copy-done.19), channel_id=1, source_target_pairs={{0,8},{8,0},{16,24},{24,16},{32,40},{40,32},{48,56},{56,48},{64,72... | collective-permute-start | bytes 786440 | tf_op jit(solution)/shard_map/ppermute | solution.py:221
  140.1 30.0 %collective-permute-start.8 = (bf16[128,1024]{1,0:T(8,128)(2,1)}, bf16[128,1024]{1,0:T(8,128)(2,1)S(1)}, u32[]{:S(2)}, u32[]{:S(2)}) collective-permute-start(bf16[128,1024]{1,0:T(8,128)(2,1)} %get-tuple-element.18), channel_id=1, source_target_pairs={{0,1},{1,2},{2,3},{3,4},{4,5},{5,6},{6,7},{7,0},{8,9},{9,10},{10,1... | collective-permute-start | bytes 786440 | tf_op jit(solution)/shard_map/ppermute | solution.py:231
  145.3 30.5 %collective-permute-start.9 = (bf16[128,1024]{1,0:T(8,128)(2,1)S(1)}, bf16[128,1024]{1,0:T(8,128)(2,1)S(1)}, u32[]{:S(2)}, u32[]{:S(2)}) collective-permute-start(bf16[128,1024]{1,0:T(8,128)(2,1)S(1)} %copy-done.23), channel_id=1, source_target_pairs={{0,9},{1,10},{2,11},{3,12},{4,13},{5,14},{6,15},{7,8},{8,1},{9,2},... | collective-permute-start | bytes 786440 | tf_op jit(solution)/shard_map/ppermute | solution.py:231
  158.2 17.5 %copy-start.13 = (bf16[128,1024]{1,0:T(8,128)(2,1)}, bf16[128,1024]{1,0:T(8,128)(2,1)S(1)}, u32[]{:S(2)}) copy-start(bf16[128,1024]{1,0:T(8,128)(2,1)S(1)} %collective-permute-done.3.near_a) | copy-start | bytes 786436
  158.2 20.5 %collective-permute-start.11 = (bf16[128,1024]{1,0:T(8,128)(2,1)S(1)}, bf16[128,1024]{1,0:T(8,128)(2,1)S(1)}, u32[]{:S(2)}, u32[]{:S(2)}) collective-permute-start(bf16[128,1024]{1,0:T(8,128)(2,1)S(1)} %copy-done.22), channel_id=1, source_target_pairs={{0,8},{8,0},{16,24},{24,16},{32,40},{40,32},{48,56},{56,48},{64,72... | collective-permute-start | bytes 786440 | tf_op jit(solution)/shard_map/ppermute | solution.py:221
  164.8 11.0 %copy-start.14 = (bf16[128,1024]{1,0:T(8,128)(2,1)}, bf16[128,1024]{1,0:T(8,128)(2,1)S(1)}, u32[]{:S(2)}) copy-start(bf16[128,1024]{1,0:T(8,128)(2,1)S(1)} %collective-permute-done.4.far_a) | copy-start | bytes 786436
  170.1 5.7 %copy-start.16 = (bf16[128,1024]{1,0:T(8,128)(2,1)}, bf16[128,1024]{1,0:T(8,128)(2,1)S(1)}, u32[]{:S(2)}) copy-start(bf16[128,1024]{1,0:T(8,128)(2,1)S(1)} %collective-permute-done.8.near_b) | copy-start | bytes 786436
  175.8 0.7 copy-start.17
  178.7 0.7 copy-start.12
  178.7 0.8 copy-start.15
  181.8 1.0 copy-start.4
